TPU v7x, 32 devices: a whole 2x2x4 slice. The times are simulated.
32 devices in a mesh: state: 16 (over z, y, core), grid: 2 (over x).
Axes of the slice: x: 2, y: 2, z: 4, core: 2. Of those that a mesh axis runs over, the one named last changes fastest.
Arguments:
- orbitals: bfloat16 [64, 32, 3584], P('state', 'grid'), may hold values from -6 to 6
- first_rotation: bfloat16 [64, 64], P(None, 'state'), may hold values from -0.75 to 0.75
- second_rotation: bfloat16 [64, 64], P(None, 'state'), may hold values from -0.75 to 0.75
- occupancy: bfloat16 [64], P('state'), may hold values from 0.1 to 6, as said below
- local_potential: float32 [32, 3584], P('grid'), may hold values from -2 to 0.5
Outputs:
- new_images: bfloat16 [64, 32, 3584], P('state', 'grid')
- density: float32 [32, 3584], P('grid')
Inputs may be any that keep to these rules, and one draw needn't show every extreme that they name: `occupancy`: positive occupations.
All inputs are finite; a program needn't handle non-finite values.
Results may differ from a plain program's by a relative error of at most 0.018.
Values may be sent and summed in bfloat16 or wider, within the bound.
A program may use at most 128 MiB of HBM per device.

v0:
```python
import jax
import jax.numpy as jnp
from jax import lax
from jax.sharding import PartitionSpec as P

GZ = 16
RADIUS = 6


stencil_weights = (
    -5369.0 / 1800.0,
    12.0 / 7.0,
    -15.0 / 56.0,
    10.0 / 189.0,
    -1.0 / 112.0,
    2.0 / 1925.0,
    -1.0 / 16632.0,
)
kinetic_scale = -0.5 / 2.25
exchange_scale = -0.9847450218426964


def extended(block, sides, width):
    for axis, dim in sides:
        count = lax.axis_size(axis)
        forward = [(i, i + 1) for i in range(count - 1)]
        backward = [(target, source) for source, target in forward]
        low = lax.ppermute(
            lax.slice_in_dim(block, block.shape[dim] - width, None, axis=dim), axis, forward
        )
        high = lax.ppermute(lax.slice_in_dim(block, 0, width, axis=dim), axis, backward)
        block = jnp.concatenate([low, block, high], axis=dim)
    return block


def contract_rows(left_block, right_block):
    return lax.dot_general(
        left_block, right_block, (((0,), (0,)), ((), ())), preferred_element_type=jnp.float32
    )


def make_potential(density, local_potential):
    return local_potential + exchange_scale * jnp.cbrt(density + 1e-06)


def operate(rotated, potential):
    planes = rotated.shape[1]
    row_length = rotated.shape[2]
    padded = extended(rotated, (("grid", 1),), RADIUS).astype(jnp.float32)
    inner_field = padded[:, RADIUS : RADIUS + planes]
    offset = RADIUS * GZ
    flat_padded = jnp.pad(inner_field, ((0, 0), (0, 0), (offset, offset)))
    depth_index = lax.broadcasted_iota(jnp.int32, (1, 1, row_length), 2) % GZ
    laplace = 3.0 * stencil_weights[0] * inner_field
    for reach in range(1, RADIUS + 1):
        weight_now = stencil_weights[reach]
        along_first = (
            padded[:, RADIUS + reach : RADIUS + reach + planes]
            + padded[:, RADIUS - reach : RADIUS - reach + planes]
        )
        along_second = (
            flat_padded[:, :, offset + reach * GZ : offset + reach * GZ + row_length]
            + flat_padded[:, :, offset - reach * GZ : offset - reach * GZ + row_length]
        )
        upper = jnp.where(
            depth_index + reach < GZ,
            flat_padded[:, :, offset + reach : offset + reach + row_length],
            0.0,
        )
        lower = jnp.where(
            depth_index - reach >= 0,
            flat_padded[:, :, offset - reach : offset - reach + row_length],
            0.0,
        )
        laplace = laplace + weight_now * (along_first + along_second + upper + lower)
    return (kinetic_scale * laplace + potential[None] * inner_field).astype(jnp.bfloat16)


def on_device(orbitals, first_rotation, second_rotation, occupancy, local_potential):
    states, planes, row_length = orbitals.shape
    all_states = first_rotation.shape[0]
    cells = planes * row_length
    flat_rows = orbitals.reshape(states, cells)
    flat_potential = local_potential.reshape(cells)
    block_rows = first_rotation
    rotated = contract_rows(
        block_rows, lax.all_gather(flat_rows, "state", axis=0, tiled=True)
    ).astype(jnp.bfloat16)
    rotated_wide = rotated.astype(jnp.float32)
    partial_density = jnp.sum(
        occupancy.astype(jnp.float32)[:, None] * rotated_wide * rotated_wide, axis=0
    )
    density = (
        lax.psum(partial_density.astype(jnp.bfloat16), "state").astype(jnp.float32) / all_states
    )
    potential = make_potential(density, flat_potential)
    images = operate(
        rotated.reshape(states, planes, row_length), potential.reshape(planes, row_length)
    )
    block_rows = second_rotation
    new_flat = contract_rows(
        block_rows, lax.all_gather(images.reshape(states, cells), "state", axis=0, tiled=True)
    ).astype(jnp.bfloat16)
    return (new_flat.reshape(states, planes, row_length), density.reshape(planes, row_length))


def solution(mesh):
    placed = (
        P("state", "grid", None),
        P(None, "state"),
        P(None, "state"),
        P("state"),
        P("grid", None),
    )
    return jax.shard_map(
        on_device,
        mesh=mesh,
        in_specs=placed,
        out_specs=(P("state", "grid", None), P("grid", None)),
        check_vma=False,
    )
```

profile of v0, /device:TPU:0, one launch (start us, length us, event | category | flops | bytes accessed | tf_op | source)
XLA Modules:
  0.0 279.9 jit_solution(4499676773396353175)
XLA Ops:
  7.2 0.0 copy-start
  7.2 0.0 all-gather.5.cloned.1.call-start
  7.2 2.1 reshape.104
  9.3 0.0 all-gather.5.cloned.1.call-update
  9.4 0.0 all-reduce.3.cloned.1.call-start
  9.4 0.7 convert_element_type.31
  10.1 1.0 reshape.100
  11.1 70.7 %all-gather.5.cloned.1.call-done = bf16[16,4,57344]{2,1,0:T(4,128)(2,1)} async-done(((bf16[1,4,57344]{2,1,0:T(4,128)(2,1)}), bf16[16,4,57344]{2,1,0:T(4,128)(2,1)}) %all-gather.5.cloned.1.call-update) | async-done | bytes 7340048 | tf_op jit(solution)/shard_map/all_gather | solution.py:87
  81.9 9.0 %reshape.105 = bf16[64,57344]{1,0:T(8,128)(2,1)} reshape(bf16[16,4,57344]{2,1,0:T(4,128)(2,1)} %all-gather.5.cloned.1.call-done) | data formatting | bytes 14680064
  90.8 0.0 copy-done
  90.8 4.9 %fusion = (bf16[57344]{0:T(1024)(128)(2,1)}, bf16[4,57344]{1,0:T(4,128)(2,1)S(1)}) fusion(f32[4]{0:T(128)S(1)} %convert_element_type.31, bf16[64,4]{0,1:T(4,128)(2,1)S(1)} %copy-done, bf16[64,57344]{1,0:T(8,128)(2,1)} %reshape.105), kind=kOutput, calls=%fused_computation.3 | convolution fusion | flops 30449664 | bytes 7914000 | tf_op jit(solution)/shard_map/dot_general | solution.py:37
  95.8 0.1 copy.12
  95.8 0.0 all-reduce.3.cloned.1.call-update
  95.9 0.0 all-gather.7.cloned.1.call-start
  95.9 0.1 fusion.52
  96.0 3.4 %collective-permute-start = (bf16[4,6,3584]{2,1,0:T(8,128)(2,1)S(1)}, bf16[4,6,3584]{2,1,0:T(8,128)(2,1)S(1)}, u32[]{:S(2)}, u32[]{:S(2)}) collective-permute-start(bf16[4,6,3584]{2,1,0:T(8,128)(2,1)S(1)} %get-tuple-element.2), channel_id=1, source_target_pairs={{0,1},{2,3},{4,5},{6,7},{8,9},{10,11},{12,13},{14,15},{16,17},{18,... | collective-permute-start | bytes 516104 | tf_op jit(solution)/shard_map/ppermute | solution.py:28
  99.4 1.3 collective-permute-start.1
  100.7 79.5 %all-reduce.3.cloned.1.call-done = bf16[57344]{0:T(1024)(128)(2,1)} async-done(((bf16[57344]{0:T(1024)(128)(2,1)}), bf16[57344]{0:T(1024)(128)(2,1)}) %all-reduce.3.cloned.1.call-update) | async-done | bytes 114704 | tf_op jit(solution)/shard_map/psum | solution.py:94
  180.2 1.1 convert_multiply_fusion
  181.3 0.0 collective-permute-done
  181.3 0.0 collective-permute-done.1
  181.3 0.3 maximum_convert_fusion
  181.7 0.1 slice.158
  181.7 5.9 %fusion.8 = bf16[4,16,3584]{2,1,0:T(8,128)(2,1)S(1)} fusion(f32[4,28,3584]{2,1,0:T(8,128)S(1)} %maximum_convert_fusion, f32[4,16,3584]{2,1,0:T(8,128)S(1)} %slice.158, f32[16,3584]{1,0:T(8,128)S(1)} %mul.96, pred[3584]{0:T(1024)(128)(4,1)S(1)} %get-tuple-element.8, pred[3584]{0:T(1024)(128)(4,1)S(1)} %get-tuple-element.9, ...), kind=kLoop, calls=%fused_computation.12 | loop fusion | flops 13533184 | bytes 12658688 | tf_op jit(solution)/shard_map/convert_element_type | solution.py:76
  187.7 1.1 reshape.106
  188.8 0.0 all-gather.7.cloned.1.call-update
  188.8 0.7 reshape.103
  189.5 0.0 copy-start.1
  189.5 69.9 %all-gather.7.cloned.1.call-done = bf16[16,4,57344]{2,1,0:T(4,128)(2,1)} async-done(((bf16[1,4,57344]{2,1,0:T(4,128)(2,1)}), bf16[16,4,57344]{2,1,0:T(4,128)(2,1)}) %all-gather.7.cloned.1.call-update) | async-done | bytes 7340048 | tf_op jit(solution)/shard_map/all_gather | solution.py:102
  259.5 9.0 %reshape.107 = bf16[64,57344]{1,0:T(8,128)(2,1)} reshape(bf16[16,4,57344]{2,1,0:T(4,128)(2,1)} %all-gather.7.cloned.1.call-done) | data formatting | bytes 14680064
  268.4 0.0 copy-done.1
  268.4 4.1 %convolution_convert_fusion = bf16[57344,4]{0,1:T(4,128)(2,1)S(1)} fusion(bf16[64,57344]{1,0:T(8,128)(2,1)} %reshape.107, bf16[64,4]{0,1:T(4,128)(2,1)S(1)} %copy-done.1), kind=kOutput, calls=%fused_computation | convolution fusion | flops 29589504 | bytes 7799296 | tf_op jit(solution)/shard_map/dot_general | solution.py:37
  272.6 0.8 copy.11
  (7 shorter events, 0.1 us)
Async XLA Ops:
  7.2 83.7 %copy-start = (bf16[64,4]{0,1:T(4,128)(2,1)S(1)}, bf16[64,4]{0,1:T(4,128)(2,1)}, u32[]{:S(2)}) copy-start(bf16[64,4]{0,1:T(4,128)(2,1)} %param.6) | copy-start | bytes 1540
  7.2 74.7 %all-gather.5.cloned.1.call-start = ((), (), s32[]{:S(2)}) async-start(), calls=%async_computation.1 | async-start | bytes 7798784 | tf_op jit(solution)/shard_map/all_gather | solution.py:87
  9.4 170.8 %all-reduce.3.cloned.1.call-start = ((), (), s32[]{:S(2)}) async-start(), calls=%async_computation | async-start | bytes 229376 | tf_op jit(solution)/shard_map/psum | solution.py:94
  95.9 163.6 %all-gather.7.cloned.1.call-start = ((), (), s32[]{:S(2)}) async-start(), calls=%async_computation.2 | async-start | bytes 7798784 | tf_op jit(solution)/shard_map/all_gather | solution.py:102
  96.0 85.3 %collective-permute-start = (bf16[4,6,3584]{2,1,0:T(8,128)(2,1)S(1)}, bf16[4,6,3584]{2,1,0:T(8,128)(2,1)S(1)}, u32[]{:S(2)}, u32[]{:S(2)}) collective-permute-start(bf16[4,6,3584]{2,1,0:T(8,128)(2,1)S(1)} %get-tuple-element.2), channel_id=1, source_target_pairs={{0,1},{2,3},{4,5},{6,7},{8,9},{10,11},{12,13},{14,15},{16,17},{18,... | collective-permute-start | bytes 516104 | tf_op jit(solution)/shard_map/ppermute | solution.py:28
  99.4 82.0 %collective-permute-start.1 = (bf16[4,6,3584]{2,1,0:T(8,128)(2,1)S(1)}, bf16[4,6,3584]{2,1,0:T(8,128)(2,1)S(1)}, u32[]{:S(2)}, u32[]{:S(2)}) collective-permute-start(bf16[4,6,3584]{2,1,0:T(8,128)(2,1)S(1)} %get-tuple-element.3), channel_id=1, source_target_pairs={{1,0},{3,2},{5,4},{7,6},{9,8},{11,10},{13,12},{15,14},{17,16},{19,... | collective-permute-start | bytes 516104 | tf_op jit(solution)/shard_map/ppermute | solution.py:31
  189.5 78.9 %copy-start.1 = (bf16[64,4]{0,1:T(4,128)(2,1)S(1)}, bf16[64,4]{0,1:T(4,128)(2,1)}, u32[]{:S(2)}) copy-start(bf16[64,4]{0,1:T(4,128)(2,1)} %param.7) | copy-start | bytes 1540
Sparse Core Ops, SparseCore 0:
  10.9 70.9 all-gather.4
  96.0 84.1 all-reduce.2
  188.9 70.4 all-gather.6
where the time goes:
time: 281 us; the launch traced here: 280 us
  waiting for transfers between devices  220 us (78%)
  local copies, waits for them, and re-layouts  23.9 us (9%)
  between operations  13.9 us (5%)
  matrix products  9.07 us (3%)
  other arithmetic  8.08 us (3%)
  starting transfers between devices  4.8 us (2%)
    psum x1, waiting for transfers between devices, on_device(): lax.psum(partial_density.astype(jnp.bfloat16), 'state').astype(jnp.float32)  79.5 us
    all_gather x1, waiting for transfers between devices, on_device(): lax.all_gather(flat_rows, 'state', axis=0, tiled=True)  70.7 us
    all_gather x1, waiting for transfers between devices, on_device(): lax.all_gather(images.reshape(states, cells), 'state', axis=0, tiled=True)  69.9 us
    unnamed x10, local copies, waits for them, and re-layouts  22.1 us
    dot_general x2, matrix products, contract_rows(): lax.dot_general(left_block, right_block, (((0,), (0,)), ((), ())), prefer...  9.07 us
    convert_element_type x1, other arithmetic, operate(): (kinetic_scale * laplace + potential[None] * inner_field).astype(jnp.bflo...  5.93 us
  transfers between devices with their start and end apart: 5, of which 3 were waited for; matrix products, arithmetic and copies ran while one was open for 1% of the time, Pallas kernels for 0%

commit v1 on v0

v1 whole, which is shorter than its diff:
```python
import functools
import jax
import jax.numpy as jnp
import numpy as np
from jax import lax
from jax.experimental import pallas as pl
from jax.experimental.pallas import tpu as pltpu
from jax.sharding import PartitionSpec as P

GZ = 16
RADIUS = 6
LANES = 128
HALO = 8

stencil_weights = (
    -5369.0 / 1800.0,
    12.0 / 7.0,
    -15.0 / 56.0,
    10.0 / 189.0,
    -1.0 / 112.0,
    2.0 / 1925.0,
    -1.0 / 16632.0,
)
kinetic_scale = -0.5 / 2.25
exchange_scale = -0.9847450218426964

F32 = jnp.float32
BF16 = jnp.bfloat16


def high_low(matrix):
    high = matrix.astype(np.float32).astype(jnp.bfloat16)
    low = (matrix - high.astype(np.float64)).astype(np.float32).astype(jnp.bfloat16)
    return np.stack([high, low])


def plane_matrix(width):
    matrix = np.zeros((width + 2 * LANES, width))
    for c in range(width):
        matrix[LANES + c, c] += 2.0 * stencil_weights[0]
        for reach in range(1, RADIUS + 1):
            for sign in (-1, 1):
                matrix[LANES + c + sign * reach * GZ, c] += stencil_weights[reach]
                if 0 <= c % GZ + sign * reach < GZ:
                    matrix[LANES + c + sign * reach, c] += stencil_weights[reach]
    return high_low(kinetic_scale * matrix)


def first_matrix(states, planes):
    own = states * planes
    matrix = np.zeros((own, own + 2 * states * HALO))
    for s in range(states):
        for p in range(planes):
            for shift in range(-RADIUS, RADIUS + 1):
                q = p + shift
                if q < 0:
                    column = own + s * HALO + HALO + q
                elif q >= planes:
                    column = own + states * HALO + s * HALO + q - planes
                else:
                    column = s * planes + q
                matrix[s * planes + p, column] += stencil_weights[abs(shift)]
    return high_low(kinetic_scale * matrix)


def halo_matrix(states, planes):
    matrix = np.zeros((2, states * HALO, states * planes), np.float32)
    for s in range(states):
        for h in range(HALO):
            matrix[0, s * HALO + h, s * planes + h] = 1.0
            matrix[1, s * HALO + h, s * planes + planes - HALO + h] = 1.0
    return matrix.astype(jnp.bfloat16)


def dot(left, right):
    return jnp.dot(left, right, preferred_element_type=F32)


def kernel(
    n, grids, workers, skip, width, total,
    psi, small, local, ymat, xmat, hmat,
    out, density_out,
    held, smalls, rot1, rot2, sent, phi, density_sent, densities, halo_sent, halos, acc,
    small_send, small_recv, psi_send, psi_recv, phi_send, phi_recv,
    density_send, density_recv, halo_send, halo_recv, own_sem,
):
    me = lax.axis_index("state")
    place = lax.axis_index("grid")
    states, planes = psi.shape[0], psi.shape[1]
    rows = total * planes
    mine = me - skip
    working = jnp.logical_and(mine >= 0, mine < workers)

    def peer(k):
        return lax.rem(me + k, n)

    def is_worker(p):
        return jnp.logical_and(p >= skip, p < skip + workers)

    def lanes(w):
        return pl.ds(pl.multiple_of(w * width, width), width)

    def small_copy(k, p, source):
        return pltpu.make_async_remote_copy(
            src_ref=small, dst_ref=smalls.at[source], send_sem=small_send.at[k],
            recv_sem=small_recv.at[source], device_id={"state": p},
            device_id_type=pl.DeviceIdType.MESH)

    def psi_copy(k, p, w, source):
        return pltpu.make_async_remote_copy(
            src_ref=psi.at[:, :, lanes(w)], dst_ref=held.at[source], send_sem=psi_send.at[k],
            recv_sem=psi_recv.at[source], device_id={"state": p},
            device_id_type=pl.DeviceIdType.MESH)

    def phi_copy(k, p, w):
        return pltpu.make_async_remote_copy(
            src_ref=sent.at[p], dst_ref=phi.at[w + 1], send_sem=phi_send.at[k],
            recv_sem=phi_recv.at[w], device_id={"state": p},
            device_id_type=pl.DeviceIdType.MESH)

    def density_copy(k, p, w):
        return pltpu.make_async_remote_copy(
            src_ref=density_sent, dst_ref=densities.at[w], send_sem=density_send.at[k],
            recv_sem=density_recv.at[w], device_id={"state": p},
            device_id_type=pl.DeviceIdType.MESH)

    def halo_copy(side, w):
        return pltpu.make_async_remote_copy(
            src_ref=halo_sent.at[side, w], dst_ref=halos.at[1 - side, w],
            send_sem=halo_send.at[side, w], recv_sem=halo_recv.at[1 - side, w],
            device_id={"grid": place - 1 if side == 0 else place + 1},
            device_id_type=pl.DeviceIdType.MESH)

    has_low = place > 0
    has_high = place < grids - 1

    barrier = pltpu.get_barrier_semaphore()

    @pl.loop(1, n)
    def _(k):
        pl.semaphore_signal(barrier, inc=1, device_id={"state": peer(k)},
                            device_id_type=pl.DeviceIdType.MESH)

    @pl.when(has_low)
    def _():
        pl.semaphore_signal(barrier, inc=1, device_id={"grid": place - 1},
                            device_id_type=pl.DeviceIdType.MESH)

    @pl.when(has_high)
    def _():
        pl.semaphore_signal(barrier, inc=1, device_id={"grid": place + 1},
                            device_id_type=pl.DeviceIdType.MESH)

    below = (place + grids - 1) // grids
    above = (2 * grids - 2 - place) // grids
    pl.semaphore_wait(barrier, n - 1 + below + above)

    @pl.loop(1, n)
    def _(k):
        p = peer(k)

        @pl.when(is_worker(p))
        def _():
            small_copy(k, p, me).start()

    @pl.loop(1, n)
    def _(k):
        p = peer(k)

        @pl.when(is_worker(p))
        def _():
            psi_copy(k, p, p - skip, me).start()

    phi[0] = jnp.zeros(phi.shape[1:], BF16)
    phi[workers + 1] = jnp.zeros(phi.shape[1:], BF16)

    @pl.when(jnp.logical_not(has_low))
    def _():
        halos[0] = jnp.zeros(halos.shape[1:], BF16)

    @pl.when(jnp.logical_not(has_high))
    def _():
        halos[1] = jnp.zeros(halos.shape[1:], BF16)

    @pl.when(working)
    def _():
        own = pltpu.make_async_copy(psi.at[:, :, lanes(mine)], held.at[me], own_sem)
        own.start()
        smalls[me] = small[...]

        @pl.loop(1, n)
        def _(k):
            small_copy(k, me, peer(k)).wait_recv()

        matrices = smalls[...].reshape(n * smalls.shape[1], LANES)
        wide = matrices.shape[0]
        row = lax.broadcasted_iota(jnp.int32, (rows, wide), 0)
        column = lax.broadcasted_iota(jnp.int32, (rows, wide), 1)
        base = (row // planes) * 4

        def repeated(which):
            pick = jnp.where(column == base + which, 1.0, 0.0).astype(BF16)
            return dot(pick, matrices)

        part = 2 * LANES
        keep = (lax.broadcasted_iota(jnp.int32, (rows, part), 0) % planes
                == lax.broadcasted_iota(jnp.int32, (rows, part), 1) % planes)
        for which, target in ((0, rot1), (1, rot2)):
            tall = repeated(which).astype(BF16)

            @pl.loop(0, rows // part)
            def _(c):
                entry = lax.broadcasted_iota(jnp.int32, (LANES, part), 0)
                at = (lax.broadcasted_iota(jnp.int32, (LANES, part), 1) + c * part) // planes
                spread = jnp.where(entry == at, 1.0, 0.0).astype(BF16)
                target[:, pl.ds(pl.multiple_of(c * part, part), part)] = jnp.where(
                    keep, dot(tall, spread), 0.0).astype(BF16)

        occupied = repeated(2)
        own.wait()

        @pl.loop(1, n)
        def _(k):
            psi_copy(k, me, mine, peer(k)).wait_recv()

        rotated = dot(rot1[...], held[...].reshape(rows, width)).astype(BF16)
        weight = jnp.concatenate([occupied] * (width // LANES), axis=1)
        squares = rotated.astype(F32)
        squares = weight * squares * squares
        density = jnp.sum(squares.reshape(total, planes, width), axis=0) / total
        density_sent[...] = density.astype(BF16)

        sent[...] = dot(rot2[...], rotated).astype(BF16).reshape(sent.shape)

        @pl.loop(1, n)
        def _(k):
            phi_copy(k, peer(k), mine).start()

        @pl.loop(1, n)
        def _(k):
            density_copy(k, peer(k), mine).start()

        phi[mine + 1] = sent[me]
        densities[mine] = density_sent[...]

    @pl.loop(0, workers)
    def _(j):
        w = lax.rem(mine + j + workers, workers)

        @pl.when(w != mine)
        def _():
            phi_copy(0, me, w).wait_recv()

        block = phi[w + 1].reshape(states * planes, width)

        @pl.when(has_low)
        def _():
            halo_sent[0, w] = dot(hmat[0], block).astype(BF16)
            halo_copy(0, w).start()

        @pl.when(has_high)
        def _():
            halo_sent[1, w] = dot(hmat[1], block).astype(BF16)
            halo_copy(1, w).start()

    flat = (workers * states * planes, -1)
    side = jnp.concatenate(
        [
            phi[0:workers, :, :, width - LANES:].reshape(flat[0], LANES),
            phi[1:workers + 1].reshape(flat[0], width),
            phi[2:workers + 2, :, :, :LANES].reshape(flat[0], LANES),
        ],
        axis=1,
    )
    acc[...] = (dot(side, ymat[0]) + dot(side, ymat[1])).reshape(acc.shape)

    @pl.loop(0, workers)
    def _(w):
        @pl.when(w != mine)
        def _():
            density_copy(0, me, w).wait_recv()

        @pl.when(has_low)
        def _():
            halo_copy(1, w).wait_recv()

        @pl.when(has_high)
        def _():
            halo_copy(0, w).wait_recv()

        density = densities[w].astype(F32)
        density_out[:, lanes(w)] = density
        potential = local[:, lanes(w)] + exchange_scale * jnp.exp(
            jnp.log(density + 1e-06) * (1.0 / 3.0))
        block = phi[w + 1]
        column = jnp.concatenate(
            [block.reshape(states * planes, width), halos[0, w], halos[1, w]], axis=0)
        kinetic = acc[w] + dot(xmat[0], column) + dot(xmat[1], column)
        result = kinetic.reshape(states, planes, width) + potential[None] * block.astype(F32)
        out[:, :, lanes(w)] = result.astype(BF16)

    @pl.loop(1, n)
    def _(k):
        p = peer(k)

        @pl.when(is_worker(p))
        def _():
            small_copy(k, p, me).wait_send()
            psi_copy(k, p, p - skip, me).wait_send()

        @pl.when(working)
        def _():
            phi_copy(k, p, mine).wait_send()
            density_copy(k, p, mine).wait_send()

    @pl.loop(0, workers)
    def _(w):
        @pl.when(has_low)
        def _():
            halo_copy(0, w).wait_send()

        @pl.when(has_high)
        def _():
            halo_copy(1, w).wait_send()


def on_device(n, grids, orbitals, first_rotation, second_rotation, occupancy, local_potential):
    states, planes, row_length = orbitals.shape
    total = first_rotation.shape[0]
    width = LANES * (-(-row_length // (LANES * n)))
    workers = row_length // width
    skip = (n - workers) // 2
    pad = ((0, 0), (0, LANES - total))
    small = jnp.stack(
        [
            jnp.pad(first_rotation.T, pad),
            jnp.pad(second_rotation.T, pad),
            jnp.broadcast_to(occupancy[:, None], (states, LANES)),
            jnp.zeros((states, LANES), BF16),
        ],
        axis=1,
    ).reshape(4 * states, LANES)
    ymat = jnp.asarray(plane_matrix(width))
    xmat = jnp.asarray(first_matrix(states, planes))
    hmat = jnp.asarray(halo_matrix(states, planes))
    vmem = pl.BlockSpec(memory_space=pltpu.VMEM)
    rows = total * planes
    dma = pltpu.SemaphoreType.DMA
    return pl.pallas_call(
        functools.partial(kernel, n, grids, workers, skip, width, total),
        out_shape=(
            jax.ShapeDtypeStruct(orbitals.shape, BF16),
            jax.ShapeDtypeStruct(local_potential.shape, F32),
        ),
        in_specs=[pl.BlockSpec(memory_space=pl.ANY)] + [vmem] * 5,
        out_specs=(vmem, vmem),
        scratch_shapes=[
            pltpu.VMEM((n, states, planes, width), BF16),
            pltpu.VMEM((n, 4 * states, LANES), BF16),
            pltpu.VMEM((rows, rows), BF16),
            pltpu.VMEM((rows, rows), BF16),
            pltpu.VMEM((n, states, planes, width), BF16),
            pltpu.VMEM((workers + 2, states, planes, width), BF16),
            pltpu.VMEM((planes, width), BF16),
            pltpu.VMEM((workers, planes, width), BF16),
            pltpu.VMEM((2, workers, states * HALO, width), BF16),
            pltpu.VMEM((2, workers, states * HALO, width), BF16),
            pltpu.VMEM((workers, states * planes, width), F32),
            dma((n,)), dma((n,)), dma((n,)), dma((n,)),
            dma((n,)), dma((workers,)), dma((n,)), dma((workers,)),
            dma((2, workers)), dma((2, workers)), dma,
        ],
        compiler_params=pltpu.CompilerParams(
            collective_id=0, has_side_effects=True, vmem_limit_bytes=56 * 1024 * 1024
        ),
        cost_estimate=pl.CostEstimate(
            flops=3_000_000_000, bytes_accessed=4_000_000, transcendentals=120_000),
    )(orbitals, small, local_potential, ymat, xmat, hmat)


def solution(mesh):
    placed = (
        P("state", "grid", None),
        P(None, "state"),
        P(None, "state"),
        P("state"),
        P("grid", None),
    )
    return jax.shard_map(
        functools.partial(on_device, mesh.shape["state"], mesh.shape["grid"]),
        mesh=mesh,
        in_specs=placed,
        out_specs=(P("state", "grid", None), P("grid", None)),
        check_vma=False,
    )
```

time: 281 us -> 47.4 us (0.17)
  the two profiles are of different devices: /device:TPU:0 before, /device:TPU:29 now
where the time goes in v1:
time: 47.4 us; the launch traced here: 47.2 us
  Pallas kernels  42 us (89%)
  local copies, waits for them, and re-layouts  4.47 us (9%)
  between operations  0.67 us (1%)
    pallas_call x1, Pallas kernels, on_device(): pl.pallas_call(functools.partial(kernel, n, grids, workers, skip, width,...  42 us
    unnamed x10, local copies, waits for them, and re-layouts  3.72 us

profile of v1, /device:TPU:29, one launch (start us, length us, event | category | flops | bytes accessed | tf_op | source)
XLA Modules:
  0.0 47.2 jit_solution(3886448759039073954)
XLA Ops:
  0.6 0.0 copy-start.3
  0.6 0.0 copy-start.2
  0.6 0.1 pad.12.clone
  0.7 0.6 %copy-done.3 = bf16[4]{0:T(256)(128)(2,1)S(1)} copy-done((bf16[4]{0:T(256)(128)(2,1)S(1)}, bf16[4]{0:T(256)(128)(2,1)}, u32[]{:S(2)}) %copy-start.3) | copy-done | bytes 32
  1.3 0.0 copy-start.1
  1.3 0.1 stack_broadcast_in_dim.8
  1.4 0.0 copy-done.2
  1.4 0.6 %copy-done.1 = bf16[64,4]{0,1:T(4,128)(2,1)S(1)} copy-done((bf16[64,4]{0,1:T(4,128)(2,1)S(1)}, bf16[64,4]{0,1:T(4,128)(2,1)}, u32[]{:S(2)}) %copy-start.1) | copy-done | bytes 536
  2.0 0.1 maximum_maximum_fusion
  2.1 0.6 %copy.10 = bf16[4,4,128]{2,1,0:T(4,128)(2,1)} copy(bf16[4,4,128]{2,0,1:T(4,128)(2,1)S(1)} %maximum_maximum_fusion) | data formatting | bytes 8192 | tf_op jit(solution)/shard_map/stack | solution.py:334
  2.7 42.0 %shard_map.95 = (bf16[4,16,3584]{2,1,0:T(8,128)(2,1)}, f32[16,3584]{1,0:T(8,128)}) custom-call(bf16[4,16,3584]{2,1,0:T(8,128)(2,1)} %psi.1, bf16[16,128]{1,0:T(8,128)(2,1)} %bitcast.8, f32[16,3584]{1,0:T(8,128)} %local.1, bf16[2,512,256]{2,1,0:T(8,128)(2,1)} %constant.10.clone.ymat, bf16[2,64,128]{2,1,0:T(8,128)(2,1)} %constant.11.clone.xmat, ...), custom_call_target="tpu_custom_call" | custom-call | flops 3000000000 | bytes 4000000 | tf_op jit(solution)/shard_map/pallas_call | solution.py:349
  44.6 0.0 copy-start
  44.7 1.9 %copy.13 = bf16[4,16,3584]{2,1,0:T(8,128)(2,1)} copy(bf16[4,16,3584]{2,1,0:T(8,128)(2,1)} %get-tuple-element.6) | data formatting | bytes 917504
  46.5 0.0 copy-done
  46.5 0.7 %copy.14 = f32[16,3584]{1,0:T(8,128)} copy(f32[16,3584]{1,0:T(8,128)S(1)} %copy-done) | data formatting | bytes 458752
  (1 shorter events, 0.0 us)
Async XLA Ops:
  0.6 0.7 %copy-start.3 = (bf16[4]{0:T(256)(128)(2,1)S(1)}, bf16[4]{0:T(256)(128)(2,1)}, u32[]{:S(2)}) copy-start(bf16[4]{0:T(256)(128)(2,1)} %param.11) | copy-start | bytes 28
  0.6 0.7 %copy-start.2 = (bf16[64,4]{0,1:T(4,128)(2,1)S(1)}, bf16[64,4]{0,1:T(4,128)(2,1)}, u32[]{:S(2)}) copy-start(bf16[64,4]{0,1:T(4,128)(2,1)} %param.9) | copy-start | bytes 1540
  1.3 0.7 %copy-start.1 = (bf16[64,4]{0,1:T(4,128)(2,1)S(1)}, bf16[64,4]{0,1:T(4,128)(2,1)}, u32[]{:S(2)}) copy-start(bf16[64,4]{0,1:T(4,128)(2,1)} %param.10) | copy-start | bytes 1540
  44.6 1.9 %copy-start = (f32[16,3584]{1,0:T(8,128)S(1)}, f32[16,3584]{1,0:T(8,128)}, u32[]{:S(2)}) copy-start(f32[16,3584]{1,0:T(8,128)} %get-tuple-element.7) | copy-start | bytes 688132

commit v2 on v1

--- a/solution.py
+++ b/solution.py
@@ -34,16 +34,16 @@
     return np.stack([high, low])
 
 
-def plane_matrix(width):
-    matrix = np.zeros((width + 2 * LANES, width))
-    for c in range(width):
+def plane_matrix():
+    matrix = np.zeros((3 * LANES, LANES))
+    for c in range(LANES):
         matrix[LANES + c, c] += 2.0 * stencil_weights[0]
         for reach in range(1, RADIUS + 1):
             for sign in (-1, 1):
                 matrix[LANES + c + sign * reach * GZ, c] += stencil_weights[reach]
                 if 0 <= c % GZ + sign * reach < GZ:
                     matrix[LANES + c + sign * reach, c] += stencil_weights[reach]
-    return high_low(kinetic_scale * matrix)
+    return np.concatenate(list(high_low(kinetic_scale * matrix)), axis=1)
 
 
 def first_matrix(states, planes):
@@ -60,7 +60,7 @@
                 else:
                     column = s * planes + q
                 matrix[s * planes + p, column] += stencil_weights[abs(shift)]
-    return high_low(kinetic_scale * matrix)
+    return np.concatenate(list(high_low(kinetic_scale * matrix)), axis=0)
 
 
 def halo_matrix(states, planes):
@@ -97,6 +97,9 @@
     def is_worker(p):
         return jnp.logical_and(p >= skip, p < skip + workers)
 
+    parts = width // LANES
+    blocks = workers * parts
+
     def lanes(w):
         return pl.ds(pl.multiple_of(w * width, width), width)
 
@@ -106,16 +109,19 @@
             recv_sem=small_recv.at[source], device_id={"state": p},
             device_id_type=pl.DeviceIdType.MESH)
 
-    def psi_copy(k, p, w, source):
+    def psi_block(w, h):
+        return psi.at[:, :, pl.ds(pl.multiple_of(w * width + h * LANES, LANES), LANES)]
+
+    def psi_copy(k, p, w, source, h):
         return pltpu.make_async_remote_copy(
-            src_ref=psi.at[:, :, lanes(w)], dst_ref=held.at[source], send_sem=psi_send.at[k],
-            recv_sem=psi_recv.at[source], device_id={"state": p},
+            src_ref=psi_block(w, h), dst_ref=held.at[h, source], send_sem=psi_send.at[h, k],
+            recv_sem=psi_recv.at[h, source], device_id={"state": p},
             device_id_type=pl.DeviceIdType.MESH)
 
-    def phi_copy(k, p, w):
+    def phi_copy(k, p, w, h):
         return pltpu.make_async_remote_copy(
-            src_ref=sent.at[p], dst_ref=phi.at[w + 1], send_sem=phi_send.at[k],
-            recv_sem=phi_recv.at[w], device_id={"state": p},
+            src_ref=sent.at[h, p], dst_ref=phi.at[w * parts + h + 1],
+            send_sem=phi_send.at[h, k], recv_sem=phi_recv.at[h, w], device_id={"state": p},
             device_id_type=pl.DeviceIdType.MESH)
 
     def density_copy(k, p, w):
@@ -124,10 +130,10 @@
             recv_sem=density_recv.at[w], device_id={"state": p},
             device_id_type=pl.DeviceIdType.MESH)
 
-    def halo_copy(side, w):
+    def halo_copy(side, h):
         return pltpu.make_async_remote_copy(
-            src_ref=halo_sent.at[side, w], dst_ref=halos.at[1 - side, w],
-            send_sem=halo_send.at[side, w], recv_sem=halo_recv.at[1 - side, w],
+            src_ref=halo_sent.at[side, h], dst_ref=halos.at[1 - side, h],
+            send_sem=halo_send.at[side, h], recv_sem=halo_recv.at[1 - side, h],
             device_id={"grid": place - 1 if side == 0 else place + 1},
             device_id_type=pl.DeviceIdType.MESH)
 
@@ -163,16 +169,17 @@
         def _():
             small_copy(k, p, me).start()
 
-    @pl.loop(1, n)
-    def _(k):
-        p = peer(k)
-
-        @pl.when(is_worker(p))
-        def _():
-            psi_copy(k, p, p - skip, me).start()
+    for h in range(parts):
+        @pl.loop(1, n)
+        def _(k):
+            p = peer(k)
+
+            @pl.when(is_worker(p))
+            def _():
+                psi_copy(k, p, p - skip, me, h).start()
 
     phi[0] = jnp.zeros(phi.shape[1:], BF16)
-    phi[workers + 1] = jnp.zeros(phi.shape[1:], BF16)
+    phi[blocks + 1] = jnp.zeros(phi.shape[1:], BF16)
 
     @pl.when(jnp.logical_not(has_low))
     def _():
@@ -184,8 +191,12 @@
 
     @pl.when(working)
     def _():
-        own = pltpu.make_async_copy(psi.at[:, :, lanes(mine)], held.at[me], own_sem)
-        own.start()
+        owns = [
+            pltpu.make_async_copy(psi_block(mine, h), held.at[h, me], own_sem.at[h])
+            for h in range(parts)
+        ]
+        for own in owns:
+            own.start()
         smalls[me] = small[...]
 
         @pl.loop(1, n)
@@ -217,62 +228,50 @@
                     keep, dot(tall, spread), 0.0).astype(BF16)
 
         occupied = repeated(2)
-        own.wait()
-
-        @pl.loop(1, n)
-        def _(k):
-            psi_copy(k, me, mine, peer(k)).wait_recv()
-
-        rotated = dot(rot1[...], held[...].reshape(rows, width)).astype(BF16)
-        weight = jnp.concatenate([occupied] * (width // LANES), axis=1)
-        squares = rotated.astype(F32)
-        squares = weight * squares * squares
-        density = jnp.sum(squares.reshape(total, planes, width), axis=0) / total
-        density_sent[...] = density.astype(BF16)
-
-        sent[...] = dot(rot2[...], rotated).astype(BF16).reshape(sent.shape)
-
-        @pl.loop(1, n)
-        def _(k):
-            phi_copy(k, peer(k), mine).start()
+        for h in range(parts):
+            owns[h].wait()
+
+            @pl.loop(1, n)
+            def _(k):
+                psi_copy(k, me, mine, peer(k), h).wait_recv()
+
+            rotated = dot(rot1[...], held[h].reshape(rows, LANES)).astype(BF16)
+            sent[h] = dot(rot2[...], rotated).astype(BF16).reshape(sent.shape[1:])
+
+            @pl.loop(1, n)
+            def _(k):
+                phi_copy(k, peer(k), mine, h).start()
+
+            squares = rotated.astype(F32)
+            squares = occupied * squares * squares
+            density = jnp.sum(squares.reshape(total, planes, LANES), axis=0) / total
+            density_sent[:, h * LANES:(h + 1) * LANES] = density.astype(BF16)
+            phi[mine * parts + h + 1] = sent[h, me]
 
         @pl.loop(1, n)
         def _(k):
             density_copy(k, peer(k), mine).start()
 
-        phi[mine + 1] = sent[me]
         densities[mine] = density_sent[...]
 
-    @pl.loop(0, workers)
-    def _(j):
-        w = lax.rem(mine + j + workers, workers)
-
-        @pl.when(w != mine)
-        def _():
-            phi_copy(0, me, w).wait_recv()
-
-        block = phi[w + 1].reshape(states * planes, width)
-
-        @pl.when(has_low)
-        def _():
-            halo_sent[0, w] = dot(hmat[0], block).astype(BF16)
-            halo_copy(0, w).start()
-
-        @pl.when(has_high)
-        def _():
-            halo_sent[1, w] = dot(hmat[1], block).astype(BF16)
-            halo_copy(1, w).start()
-
-    flat = (workers * states * planes, -1)
-    side = jnp.concatenate(
-        [
-            phi[0:workers, :, :, width - LANES:].reshape(flat[0], LANES),
-            phi[1:workers + 1].reshape(flat[0], width),
-            phi[2:workers + 2, :, :, :LANES].reshape(flat[0], LANES),
-        ],
-        axis=1,
-    )
-    acc[...] = (dot(side, ymat[0]) + dot(side, ymat[1])).reshape(acc.shape)
+    own_rows = states * planes
+    for h in range(parts):
+        @pl.loop(0, workers)
+        def _(w):
+            @pl.when(w != mine)
+            def _():
+                phi_copy(0, me, w, h).wait_recv()
+
+        for side, present in ((0, has_low), (1, has_high)):
+            @pl.when(present)
+            def _():
+                half = jnp.concatenate(
+                    [phi[w * parts + h + 1].reshape(own_rows, LANES) for w in range(workers)],
+                    axis=1)
+                outer = dot(hmat[side], half).astype(BF16)
+                for w in range(workers):
+                    halo_sent[side, h, w] = outer[:, w * LANES:(w + 1) * LANES]
+                halo_copy(side, h).start()
 
     @pl.loop(0, workers)
     def _(w):
@@ -280,24 +279,50 @@
         def _():
             density_copy(0, me, w).wait_recv()
 
+    group = 2
+    span = group * parts
+
+    @pl.loop(0, workers // group)
+    def _(g):
+        first = g * span
+        side = jnp.concatenate(
+            [phi[pl.ds(first + shift, span)].reshape(span * own_rows, LANES)
+             for shift in range(3)], axis=1)
+        both = dot(side, ymat[...])
+        both = (both[:, :LANES] + both[:, LANES:]).reshape(span, own_rows, LANES)
+        kinetic = jnp.concatenate([both[i] for i in range(span)], axis=1)
+        middle = phi[pl.ds(first + 1, span)].reshape(span, own_rows, LANES)
+        block = jnp.concatenate([middle[i] for i in range(span)], axis=1)
+        across = dot(xmat[:, :own_rows], block)
+        kinetic = kinetic + (across[:own_rows] + across[own_rows:])
+        arrived = densities[pl.ds(g * group, group)]
+        density = jnp.concatenate([arrived[i] for i in range(group)], axis=1).astype(F32)
+        at = pl.ds(pl.multiple_of(g * span * LANES, span * LANES), span * LANES)
+        density_out[:, at] = density
+        potential = local[:, at] + exchange_scale * jnp.exp(
+            jnp.log(density + 1e-06) * (1.0 / 3.0))
+        acc[g] = kinetic.reshape(states, planes, span * LANES) + (
+            potential[None] * block.astype(F32).reshape(states, planes, span * LANES))
+
+    for h in range(parts):
         @pl.when(has_low)
         def _():
-            halo_copy(1, w).wait_recv()
+            halo_copy(1, h).wait_recv()
 
         @pl.when(has_high)
         def _():
-            halo_copy(0, w).wait_recv()
-
-        density = densities[w].astype(F32)
-        density_out[:, lanes(w)] = density
-        potential = local[:, lanes(w)] + exchange_scale * jnp.exp(
-            jnp.log(density + 1e-06) * (1.0 / 3.0))
-        block = phi[w + 1]
-        column = jnp.concatenate(
-            [block.reshape(states * planes, width), halos[0, w], halos[1, w]], axis=0)
-        kinetic = acc[w] + dot(xmat[0], column) + dot(xmat[1], column)
-        result = kinetic.reshape(states, planes, width) + potential[None] * block.astype(F32)
-        out[:, :, lanes(w)] = result.astype(BF16)
+            halo_copy(0, h).wait_recv()
+
+    @pl.loop(0, workers // group)
+    def _(g):
+        outer = jnp.concatenate(
+            [jnp.concatenate([halos[0, h, g * group + i], halos[1, h, g * group + i]], axis=0)
+             for i in range(group) for h in range(parts)], axis=1)
+        across = dot(xmat[:, own_rows:], outer)
+        across = (across[:own_rows] + across[own_rows:]).reshape(
+            states, planes, span * LANES)
+        at = pl.ds(pl.multiple_of(g * span * LANES, span * LANES), span * LANES)
+        out[:, :, at] = (acc[g] + across).astype(BF16)
 
     @pl.loop(1, n)
     def _(k):
@@ -306,22 +331,23 @@
         @pl.when(is_worker(p))
         def _():
             small_copy(k, p, me).wait_send()
-            psi_copy(k, p, p - skip, me).wait_send()
+            for h in range(parts):
+                psi_copy(k, p, p - skip, me, h).wait_send()
 
         @pl.when(working)
         def _():
-            phi_copy(k, p, mine).wait_send()
+            for h in range(parts):
+                phi_copy(k, p, mine, h).wait_send()
             density_copy(k, p, mine).wait_send()
 
-    @pl.loop(0, workers)
-    def _(w):
+    for h in range(parts):
         @pl.when(has_low)
         def _():
-            halo_copy(0, w).wait_send()
+            halo_copy(0, h).wait_send()
 
         @pl.when(has_high)
         def _():
-            halo_copy(1, w).wait_send()
+            halo_copy(1, h).wait_send()
 
 
 def on_device(n, grids, orbitals, first_rotation, second_rotation, occupancy, local_potential):
@@ -329,6 +355,7 @@
     total = first_rotation.shape[0]
     width = LANES * (-(-row_length // (LANES * n)))
     workers = row_length // width
+    parts = width // LANES
     skip = (n - workers) // 2
     pad = ((0, 0), (0, LANES - total))
     small = jnp.stack(
@@ -340,7 +367,7 @@
         ],
         axis=1,
     ).reshape(4 * states, LANES)
-    ymat = jnp.asarray(plane_matrix(width))
+    ymat = jnp.asarray(plane_matrix())
     xmat = jnp.asarray(first_matrix(states, planes))
     hmat = jnp.asarray(halo_matrix(states, planes))
     vmem = pl.BlockSpec(memory_space=pltpu.VMEM)
@@ -355,20 +382,20 @@
         in_specs=[pl.BlockSpec(memory_space=pl.ANY)] + [vmem] * 5,
         out_specs=(vmem, vmem),
         scratch_shapes=[
-            pltpu.VMEM((n, states, planes, width), BF16),
+            pltpu.VMEM((parts, n, states, planes, LANES), BF16),
             pltpu.VMEM((n, 4 * states, LANES), BF16),
             pltpu.VMEM((rows, rows), BF16),
             pltpu.VMEM((rows, rows), BF16),
-            pltpu.VMEM((n, states, planes, width), BF16),
-            pltpu.VMEM((workers + 2, states, planes, width), BF16),
+            pltpu.VMEM((parts, n, states, planes, LANES), BF16),
+            pltpu.VMEM((workers * parts + 2, states, planes, LANES), BF16),
             pltpu.VMEM((planes, width), BF16),
             pltpu.VMEM((workers, planes, width), BF16),
-            pltpu.VMEM((2, workers, states * HALO, width), BF16),
-            pltpu.VMEM((2, workers, states * HALO, width), BF16),
-            pltpu.VMEM((workers, states * planes, width), F32),
-            dma((n,)), dma((n,)), dma((n,)), dma((n,)),
-            dma((n,)), dma((workers,)), dma((n,)), dma((workers,)),
-            dma((2, workers)), dma((2, workers)), dma,
+            pltpu.VMEM((2, parts, workers, states * HALO, LANES), BF16),
+            pltpu.VMEM((2, parts, workers, states * HALO, LANES), BF16),
+            pltpu.VMEM((workers // 2, states, planes, 2 * width), F32),
+            dma((n,)), dma((n,)), dma((parts, n)), dma((parts, n)),
+            dma((parts, n)), dma((parts, workers)), dma((n,)), dma((workers,)),
+            dma((2, parts)), dma((2, parts)), dma((parts,)),
         ],
         compiler_params=pltpu.CompilerParams(
             collective_id=0, has_side_effects=True, vmem_limit_bytes=56 * 1024 * 1024

time: 47.4 us -> 44.9 us (0.947)
  the two profiles are of different devices: /device:TPU:29 before, /device:TPU:0 now
where the time goes in v2:
time: 44.9 us; the launch traced here: 44.2 us
  Pallas kernels  39 us (87%)
  local copies, waits for them, and re-layouts  4.47 us (10%)
  between operations  0.67 us (1%)
    pallas_call x1, Pallas kernels, on_device(): pl.pallas_call(functools.partial(kernel, n, grids, workers, skip, width,...  39 us
    unnamed x10, local copies, waits for them, and re-layouts  3.72 us

profile of v2, /device:TPU:0, one launch (start us, length us, event | category | flops | bytes accessed | tf_op | source)
XLA Modules:
  0.0 44.2 jit_solution(9469050273962224493)
XLA Ops:
  0.6 0.0 copy-start.3
  0.6 0.0 copy-start.2
  0.6 0.1 pad.12.clone
  0.7 0.6 %copy-done.3 = bf16[4]{0:T(256)(128)(2,1)S(1)} copy-done((bf16[4]{0:T(256)(128)(2,1)S(1)}, bf16[4]{0:T(256)(128)(2,1)}, u32[]{:S(2)}) %copy-start.3) | copy-done | bytes 32
  1.3 0.0 copy-start.1
  1.3 0.1 stack_broadcast_in_dim.8
  1.4 0.0 copy-done.2
  1.4 0.6 %copy-done.1 = bf16[64,4]{0,1:T(4,128)(2,1)S(1)} copy-done((bf16[64,4]{0,1:T(4,128)(2,1)S(1)}, bf16[64,4]{0,1:T(4,128)(2,1)}, u32[]{:S(2)}) %copy-start.1) | copy-done | bytes 536
  2.0 0.1 maximum_maximum_fusion
  2.1 0.6 %copy.10 = bf16[4,4,128]{2,1,0:T(4,128)(2,1)} copy(bf16[4,4,128]{2,0,1:T(4,128)(2,1)S(1)} %maximum_maximum_fusion) | data formatting | bytes 8192 | tf_op jit(solution)/shard_map/stack | solution.py:361
  2.7 39.0 %shard_map.95 = (bf16[4,16,3584]{2,1,0:T(8,128)(2,1)}, f32[16,3584]{1,0:T(8,128)}) custom-call(bf16[4,16,3584]{2,1,0:T(8,128)(2,1)} %psi.1, bf16[16,128]{1,0:T(8,128)(2,1)} %bitcast.8, f32[16,3584]{1,0:T(8,128)} %local.1, bf16[384,256]{1,0:T(8,128)(2,1)} %constant.10.clone.ymat, bf16[128,128]{1,0:T(8,128)(2,1)} %constant.11.clone.xmat, ...), custom_call_target="tpu_custom_call" | custom-call | flops 3000000000 | bytes 4000000 | tf_op jit(solution)/shard_map/pallas_call | solution.py:376
  41.6 0.0 copy-start
  41.6 1.9 %copy.13 = bf16[4,16,3584]{2,1,0:T(8,128)(2,1)} copy(bf16[4,16,3584]{2,1,0:T(8,128)(2,1)} %get-tuple-element.6) | data formatting | bytes 917504
  43.5 0.0 copy-done
  43.5 0.7 %copy.14 = f32[16,3584]{1,0:T(8,128)} copy(f32[16,3584]{1,0:T(8,128)S(1)} %copy-done) | data formatting | bytes 458752
  (1 shorter events, 0.0 us)
Async XLA Ops:
  0.6 0.7 %copy-start.3 = (bf16[4]{0:T(256)(128)(2,1)S(1)}, bf16[4]{0:T(256)(128)(2,1)}, u32[]{:S(2)}) copy-start(bf16[4]{0:T(256)(128)(2,1)} %param.11) | copy-start | bytes 28
  0.6 0.7 %copy-start.2 = (bf16[64,4]{0,1:T(4,128)(2,1)S(1)}, bf16[64,4]{0,1:T(4,128)(2,1)}, u32[]{:S(2)}) copy-start(bf16[64,4]{0,1:T(4,128)(2,1)} %param.9) | copy-start | bytes 1540
  1.3 0.7 %copy-start.1 = (bf16[64,4]{0,1:T(4,128)(2,1)S(1)}, bf16[64,4]{0,1:T(4,128)(2,1)}, u32[]{:S(2)}) copy-start(bf16[64,4]{0,1:T(4,128)(2,1)} %param.10) | copy-start | bytes 1540
  41.6 1.9 %copy-start = (f32[16,3584]{1,0:T(8,128)S(1)}, f32[16,3584]{1,0:T(8,128)}, u32[]{:S(2)}) copy-start(f32[16,3584]{1,0:T(8,128)} %get-tuple-element.7) | copy-start | bytes 688132

commit v3 on v2

--- a/solution.py
+++ b/solution.py
@@ -82,7 +82,7 @@
     out, density_out,
     held, smalls, rot1, rot2, sent, phi, density_sent, densities, halo_sent, halos, acc,
     small_send, small_recv, psi_send, psi_recv, phi_send, phi_recv,
-    density_send, density_recv, halo_send, halo_recv, own_sem,
+    density_send, density_recv, forward_send, halo_send, halo_recv, own_sem,
 ):
     me = lax.axis_index("state")
     place = lax.axis_index("grid")
@@ -129,6 +129,15 @@
             src_ref=density_sent, dst_ref=densities.at[w], send_sem=density_send.at[k],
             recv_sem=density_recv.at[w], device_id={"state": p},
             device_id_type=pl.DeviceIdType.MESH)
+
+    def forward_copy(w):
+        return pltpu.make_async_remote_copy(
+            src_ref=densities.at[w], dst_ref=densities.at[w], send_sem=forward_send.at[w],
+            recv_sem=density_recv.at[w], device_id={"state": me + 1 - 2 * lax.rem(me, 2)},
+            device_id_type=pl.DeviceIdType.MESH)
+
+    def same_core(w):
+        return lax.rem(w + skip, 2) == lax.rem(me, 2)
 
     def halo_copy(side, h):
         return pltpu.make_async_remote_copy(
@@ -236,26 +245,38 @@
                 psi_copy(k, me, mine, peer(k), h).wait_recv()
 
             rotated = dot(rot1[...], held[h].reshape(rows, LANES)).astype(BF16)
-            sent[h] = dot(rot2[...], rotated).astype(BF16).reshape(sent.shape[1:])
-
-            @pl.loop(1, n)
-            def _(k):
-                phi_copy(k, peer(k), mine, h).start()
-
             squares = rotated.astype(F32)
             squares = occupied * squares * squares
             density = jnp.sum(squares.reshape(total, planes, LANES), axis=0) / total
             density_sent[:, h * LANES:(h + 1) * LANES] = density.astype(BF16)
+            if h == parts - 1:
+                densities[mine] = density_sent[...]
+
+                @pl.loop(1, n // 2)
+                def _(k):
+                    density_copy(2 * k, peer(2 * k), mine).start()
+
+            sent[h] = dot(rot2[...], rotated).astype(BF16).reshape(sent.shape[1:])
+
+            @pl.loop(1, n)
+            def _(k):
+                phi_copy(k, peer(k), mine, h).start()
+
             phi[mine * parts + h + 1] = sent[h, me]
-
-        @pl.loop(1, n)
-        def _(k):
-            density_copy(k, peer(k), mine).start()
-
-        densities[mine] = density_sent[...]
 
     own_rows = states * planes
     for h in range(parts):
+        if h == parts - 1:
+            @pl.loop(0, workers)
+            def _(w):
+                @pl.when(same_core(w))
+                def _():
+                    @pl.when(w != mine)
+                    def _():
+                        density_copy(0, me, w).wait_recv()
+
+                    forward_copy(w).start()
+
         @pl.loop(0, workers)
         def _(w):
             @pl.when(w != mine)
@@ -275,9 +296,9 @@
 
     @pl.loop(0, workers)
     def _(w):
-        @pl.when(w != mine)
-        def _():
-            density_copy(0, me, w).wait_recv()
+        @pl.when(jnp.logical_not(same_core(w)))
+        def _():
+            forward_copy(w).wait_recv()
 
     group = 2
     span = group * parts
@@ -338,7 +359,16 @@
         def _():
             for h in range(parts):
                 phi_copy(k, p, mine, h).wait_send()
-            density_copy(k, p, mine).wait_send()
+
+            @pl.when(lax.rem(k, 2) == 0)
+            def _():
+                density_copy(k, p, mine).wait_send()
+
+    @pl.loop(0, workers)
+    def _(w):
+        @pl.when(same_core(w))
+        def _():
+            forward_copy(w).wait_send()
 
     for h in range(parts):
         @pl.when(has_low)
@@ -394,7 +424,7 @@
             pltpu.VMEM((2, parts, workers, states * HALO, LANES), BF16),
             pltpu.VMEM((workers // 2, states, planes, 2 * width), F32),
             dma((n,)), dma((n,)), dma((parts, n)), dma((parts, n)),
-            dma((parts, n)), dma((parts, workers)), dma((n,)), dma((workers,)),
+            dma((parts, n)), dma((parts, workers)), dma((n,)), dma((workers,)), dma((workers,)),
             dma((2, parts)), dma((2, parts)), dma((parts,)),
         ],
         compiler_params=pltpu.CompilerParams(

time: 44.9 us -> 45.3 us (level); the launches traced: 44.2 us -> 45.1 us
  Pallas kernels: 39 us -> 39.9 us
    pallas_call x1, Pallas kernels: 39 us -> 39.9 us  [on_device(): pl.pallas_call(functools.partial(kernel, n, grids, workers, skip, width,...]
where the time goes in v3:
time: 45.3 us; the launch traced here: 45.1 us
  Pallas kernels  39.9 us (88%)
  local copies, waits for them, and re-layouts  4.47 us (10%)
  between operations  0.67 us (1%)
    pallas_call x1, Pallas kernels, on_device(): pl.pallas_call(functools.partial(kernel, n, grids, workers, skip, width,...  39.9 us
    unnamed x10, local copies, waits for them, and re-layouts  3.72 us

profile of v3, /device:TPU:0, one launch (start us, length us, event | category | flops | bytes accessed | tf_op | source)
XLA Modules:
  0.0 45.1 jit_solution(16496922069028946119)
XLA Ops:
  0.6 0.0 copy-start.3
  0.6 0.0 copy-start.2
  0.6 0.1 pad.12.clone
  0.7 0.6 %copy-done.3 = bf16[4]{0:T(256)(128)(2,1)S(1)} copy-done((bf16[4]{0:T(256)(128)(2,1)S(1)}, bf16[4]{0:T(256)(128)(2,1)}, u32[]{:S(2)}) %copy-start.3) | copy-done | bytes 32
  1.3 0.0 copy-start.1
  1.3 0.1 stack_broadcast_in_dim.8
  1.4 0.0 copy-done.2
  1.4 0.6 %copy-done.1 = bf16[64,4]{0,1:T(4,128)(2,1)S(1)} copy-done((bf16[64,4]{0,1:T(4,128)(2,1)S(1)}, bf16[64,4]{0,1:T(4,128)(2,1)}, u32[]{:S(2)}) %copy-start.1) | copy-done | bytes 536
  2.0 0.1 maximum_maximum_fusion
  2.1 0.6 %copy.10 = bf16[4,4,128]{2,1,0:T(4,128)(2,1)} copy(bf16[4,4,128]{2,0,1:T(4,128)(2,1)S(1)} %maximum_maximum_fusion) | data formatting | bytes 8192 | tf_op jit(solution)/shard_map/stack | solution.py:391
  2.7 39.9 %shard_map.95 = (bf16[4,16,3584]{2,1,0:T(8,128)(2,1)}, f32[16,3584]{1,0:T(8,128)}) custom-call(bf16[4,16,3584]{2,1,0:T(8,128)(2,1)} %psi.1, bf16[16,128]{1,0:T(8,128)(2,1)} %bitcast.8, f32[16,3584]{1,0:T(8,128)} %local.1, bf16[384,256]{1,0:T(8,128)(2,1)} %constant.10.clone.ymat, bf16[128,128]{1,0:T(8,128)(2,1)} %constant.11.clone.xmat, ...), custom_call_target="tpu_custom_call" | custom-call | flops 3000000000 | bytes 4000000 | tf_op jit(solution)/shard_map/pallas_call | solution.py:406
  42.6 0.0 copy-start
  42.6 1.9 %copy.13 = bf16[4,16,3584]{2,1,0:T(8,128)(2,1)} copy(bf16[4,16,3584]{2,1,0:T(8,128)(2,1)} %get-tuple-element.6) | data formatting | bytes 917504
  44.5 0.0 copy-done
  44.5 0.7 %copy.14 = f32[16,3584]{1,0:T(8,128)} copy(f32[16,3584]{1,0:T(8,128)S(1)} %copy-done) | data formatting | bytes 458752
  (1 shorter events, 0.0 us)
Async XLA Ops:
  0.6 0.7 %copy-start.3 = (bf16[4]{0:T(256)(128)(2,1)S(1)}, bf16[4]{0:T(256)(128)(2,1)}, u32[]{:S(2)}) copy-start(bf16[4]{0:T(256)(128)(2,1)} %param.11) | copy-start | bytes 28
  0.6 0.7 %copy-start.2 = (bf16[64,4]{0,1:T(4,128)(2,1)S(1)}, bf16[64,4]{0,1:T(4,128)(2,1)}, u32[]{:S(2)}) copy-start(bf16[64,4]{0,1:T(4,128)(2,1)} %param.9) | copy-start | bytes 1540
  1.3 0.7 %copy-start.1 = (bf16[64,4]{0,1:T(4,128)(2,1)S(1)}, bf16[64,4]{0,1:T(4,128)(2,1)}, u32[]{:S(2)}) copy-start(bf16[64,4]{0,1:T(4,128)(2,1)} %param.10) | copy-start | bytes 1540
  42.6 1.9 %copy-start = (f32[16,3584]{1,0:T(8,128)S(1)}, f32[16,3584]{1,0:T(8,128)}, u32[]{:S(2)}) copy-start(f32[16,3584]{1,0:T(8,128)} %get-tuple-element.7) | copy-start | bytes 688132
